TPU v7x, 32 devices: a whole 2x2x4 slice. The times are simulated.
32 devices in a mesh: groups: 2 (over y), leaf: 4 (over z), rhs: 2 (over x), half: 2 (over core).
Axes of the slice: x: 2, y: 2, z: 4, core: 2. Of those that a mesh axis runs over, the one named last changes fastest.
Arguments:
- sources: bfloat16 [2, 32, 16384], P(None, 'rhs', ('groups', 'leaf', 'half')), parts along dimension 2, may hold values from -6 to 6
- probe_field: bfloat16 [2, 32, 16384], P(None, 'rhs', ('groups', 'leaf', 'half')), parts along dimension 2, may hold values from -6 to 6
- factor_weight: bfloat16 [6, 128, 2, 2, 128, 128], P(None, ('groups', 'leaf', 'half')), parts along dimension 1, may hold values from -0.25 to 0.25
- factor_pattern: int32 [6, 128, 2], P(None, ('groups', 'leaf', 'half')), parts along dimension 1, may hold values from 0 to 15, as said below
- near_weight: bfloat16 [128, 2, 2, 128, 128], P(('groups', 'leaf', 'half'), 'rhs'), parts along dimension 0, may hold values from -0.25 to 0.25
- near_index: int32 [128, 2], P(('groups', 'leaf', 'half')), parts along dimension 0, may hold values from 0 to 7
- tree_order: int32 [16384], P(('groups', 'leaf', 'half')), parts along dimension 0, may hold values from 0 to 1023, as said below
Outputs:
- forward_field: bfloat16 [2, 32, 16384], P(None, 'rhs', ('groups', 'leaf', 'half')), parts along dimension 2
- adjoint_field: bfloat16 [2, 32, 16384], P(None, 'rhs', ('groups', 'leaf', 'half')), parts along dimension 2
There are 2 independent parts, one for each index of `groups`. A program takes and returns all parts, laid end to end along the dimension named above; each array names one. Nothing has to cross between parts.
Inputs may be any that keep to these rules, and one draw needn't show every extreme that they name: `factor_pattern`: at levels below 3 every entry is below 8 (a block of the same cluster); at higher levels an entry below 8 names a block of the same cluster and an entry p of 8 or more names block p - 8 of the partner cluster. `tree_order`: each aligned run of 1024 entries (one cluster) is a permutation of 0 to 1023.
All inputs are finite; a program needn't handle non-finite values.
Results may differ from a plain program's by a relative error of at most 0.017.
Values may be sent and summed in bfloat16 or wider, within the bound.
A program may use at most 64 MiB of HBM per device.

v0:
```python
import jax
import jax.numpy as jnp
from jax import lax
from jax.sharding import PartitionSpec as P

BLK = 128
LOC = 3


def partner_2(value, axis, bit):
    mask = 2**bit
    pairs = [(source, source ^ mask) for source in range(lax.axis_size(axis))]
    return lax.ppermute(value, axis, pairs)


def apply_blocks(candidates, weights, chosen_slots):
    chosen = jnp.take(candidates, chosen_slots, axis=2)

    def product(left_part, right_part):
        return jnp.einsum(
            "cgkr,gksr->cgs", left_part, right_part, preferred_element_type=jnp.float32
        )

    real_part = product(chosen[0], weights[:, :, 0]) - product(chosen[1], weights[:, :, 1])
    imag_part = product(chosen[1], weights[:, :, 0]) + product(chosen[0], weights[:, :, 1])
    return jnp.stack([real_part, imag_part])


def spread_blocks(current, weights, chosen_slots, slot_count):

    def product(left_part, right_part):
        return jnp.einsum(
            "cgs,gksr->cgkr", left_part, right_part, preferred_element_type=jnp.float32
        )

    real_part = product(current[0], weights[:, :, 0]) + product(current[1], weights[:, :, 1])
    imag_part = product(current[1], weights[:, :, 0]) - product(current[0], weights[:, :, 1])
    contrib = jnp.stack([real_part, imag_part])
    onehot = (
        chosen_slots[:, :, None] == jnp.arange(slot_count, dtype=jnp.int32)[None, None, :]
    ).astype(jnp.float32)
    return jnp.einsum("zcgkr,gkt->zctr", contrib, onehot, precision=lax.Precision.HIGHEST)


def body(sources, probe_field, factor_weight, factor_pattern, near_weight, near_index, tree_order):
    columns = sources.shape[1]
    local_rows = sources.shape[2]
    count_blocks = local_rows // BLK
    x_tree = jnp.take(sources, tree_order, axis=2)
    v_tree = jnp.take(probe_field, tree_order, axis=2)
    block_shape = (2, columns, count_blocks, BLK)
    levels = factor_weight.shape[0]
    current = x_tree.reshape(block_shape)
    for level_id in range(levels):
        chosen_slots = factor_pattern[level_id]
        if level_id < LOC:
            candidates = current
        else:
            partner = partner_2(current, ("leaf", "half"), level_id - LOC)
            candidates = jnp.concatenate([current, partner], axis=2)
        current = apply_blocks(candidates, factor_weight[level_id], chosen_slots).astype(
            jnp.bfloat16
        )
    far_forward = current
    current = v_tree.reshape(block_shape)
    for level_id in reversed(range(levels)):
        chosen_slots = factor_pattern[level_id]
        if level_id < LOC:
            current = spread_blocks(
                current, factor_weight[level_id], chosen_slots, count_blocks
            ).astype(jnp.bfloat16)
        else:
            summed = spread_blocks(current, factor_weight[level_id], chosen_slots, 2 * count_blocks)
            arrived = partner_2(
                summed[:, :, count_blocks:].astype(jnp.bfloat16), ("leaf", "half"), level_id - LOC
            ).astype(jnp.float32)
            current = (summed[:, :, :count_blocks] + arrived).astype(jnp.bfloat16)
    all_weight = lax.all_gather(near_weight, "rhs", axis=1, tiled=True)
    near_forward = apply_blocks(x_tree.reshape(block_shape), all_weight, near_index)
    near_adjoint = spread_blocks(v_tree.reshape(block_shape), all_weight, near_index, count_blocks)
    out_shape = (2, columns, local_rows)
    forward_tree = (
        (far_forward.astype(jnp.float32) + near_forward).astype(jnp.bfloat16).reshape(out_shape)
    )
    adjoint_tree = (
        (current.astype(jnp.float32) + near_adjoint).astype(jnp.bfloat16).reshape(out_shape)
    )
    forward_field = jnp.zeros_like(sources).at[:, :, tree_order].set(forward_tree)
    adjoint_field = jnp.zeros_like(sources).at[:, :, tree_order].set(adjoint_tree)
    return (forward_field, adjoint_field)


def solution(mesh):
    return jax.shard_map(
        body,
        mesh=mesh,
        in_specs=(
            P(None, "rhs", ("groups", "leaf", "half")),
            P(None, "rhs", ("groups", "leaf", "half")),
            P(None, ("groups", "leaf", "half"), None, None, None, None),
            P(None, ("groups", "leaf", "half"), None),
            P(("groups", "leaf", "half"), "rhs", None, None, None),
            P(("groups", "leaf", "half"), None),
            P(("groups", "leaf", "half")),
        ),
        out_specs=(
            P(None, "rhs", ("groups", "leaf", "half")),
            P(None, "rhs", ("groups", "leaf", "half")),
        ),
        check_vma=False,
    )
```

profile of v0, /device:TPU:0, one launch (start us, length us, event | category | flops | bytes accessed | tf_op | source)
XLA Modules:
  0.0 175.3 jit_solution(16006921813619124813)
XLA Ops:
  7.2 0.7 broadcast_clamp_fusion
  7.9 0.7 compare_and_fusion
  8.6 5.3 %fusion.144 = (bf16[1,8,2,2,128,128]{5,4,3,2,1,0:T(8,128)(2,1)S(1)}, bf16[1,8,2,2,128,128]{5,4,3,2,1,0:T(8,128)(2,1)}, bf16[1,8,2,2,128,128]{5,4,3,2,1,0:T(8,128...) fusion(bf16[6,8,2,2,128,128]{5,4,3,2,1,0:T(8,128)(2,1)} %param.15), kind=kLoop, calls=%fused_computation.309 | loop fusion | bytes 12582912 | tf_op jit(solution)/shard_map/slice | solution.py:61
  14.7 3.7 %gather_fusion.8 = bf16[1024,2,16]{2,1,0:T(2,128)(2,1)S(1)} fusion(bf16[2,16,1024]{1,0,2:T(2,128)(2,1)S(1)} %copy.101, s32[1024]{0:T(1024)S(1)} %get-tuple-element.45), kind=kCustom, calls=%fused_computation.3.clone | custom fusion | bytes 135168 | tf_op jit(solution)/shard_map/jit(_take)/gather | solution.py:50
  18.4 3.7 %gather_fusion = bf16[1024,2,16]{2,1,0:T(2,128)(2,1)S(1)} fusion(bf16[2,16,1024]{1,0,2:T(2,128)(2,1)S(1)} %copy.71, s32[1024]{0:T(1024)S(1)} %get-tuple-element.45), kind=kCustom, calls=%fused_computation.clone | custom fusion | bytes 135168 | tf_op jit(solution)/shard_map/jit(_take)/gather | solution.py:49
  22.1 4.5 %fusion.63 = (bf16[2,16,1024]{1,0,2:T(2,128)(2,1)S(1)}, bf16[1024,2,16]{2,1,0:T(2,128)(2,1)}) fusion(bf16[1024,2,16]{2,1,0:T(2,128)(2,1)S(1)} %gather_fusion.8, pred[1024]{0:T(1024)(128)(4,1)S(1)} %compare_and_fusion, bf16[1024,2,16]{2,1,0:T(2,128)(2,1)S(1)} %gather_fusion), kind=kLoop, calls=%fused_computation.145 | loop fusion | flops 65536 | bytes 263168 | tf_op jit(solution)/shard_map/jit(_take)/select_n | solution.py:50
  26.5 0.7 fusion.145
  27.8 1.7 copy_bitcast_fusion
  30.3 0.6 slice_bitcast_fusion.127
  31.4 0.7 slice.551
  32.1 4.0 %collective-permute-start.3 = (bf16[2,16,8,128]{3,2,1,0:T(8,128)(2,1)}, bf16[2,16,8,128]{3,2,1,0:T(8,128)(2,1)}, u32[]{:S(2)}, u32[]{:S(2)}) collective-permute-start(bf16[2,16,8,128]{3,2,1,0:T(8,128)(2,1)} %slice.551), channel_id=1, source_target_pairs={{0,8},{1,9},{4,12},{5,13},{8,0},{9,1},{12,4},{13,5},{2,10},{3,11},... | collective-permute-start | bytes 196616 | tf_op jit(solution)/shard_map/ppermute | solution.py:13
  36.2 1.9 %copy.97 = bf16[8,1,2,128,128]{4,3,1,0,2:T(8,128)(2,1)} copy(bf16[8,1,2,128,128]{4,3,2,1,0:T(8,128)(2,1)} %param.17) | data formatting | bytes 1048576 | tf_op args[4]
  39.3 1.4 copy.73
  44.2 1.3 copy.370
  48.0 0.7 pad_maximum_fusion.12
  48.7 1.3 copy.368
  50.0 2.3 %copy.369 = bf16[1,8,2,2,128,128]{5,4,2,1,3,0:T(8,128)(2,1)} copy(bf16[1,8,2,2,128,128]{5,4,3,2,1,0:T(8,128)(2,1)} %get-tuple-element.11) | data formatting | bytes 2097152
  52.5 1.2 copy.67
  53.9 1.2 copy.66
  55.1 0.7 copy.88
  55.8 0.7 reshape.180
  56.5 1.3 copy.65
  58.0 1.2 gather_fusion.7
  59.2 0.9 copy.96
  60.3 0.7 pad_clamp_fusion.1
  61.0 0.9 pad_maximum_fusion.7
  61.9 1.2 gather_fusion.4
  63.1 1.0 fusion.91
  64.1 1.3 convolution_bitcast_fusion.22
  65.4 1.3 convolution_bitcast_fusion.20
  66.7 0.9 fusion.87
  68.4 1.3 fusion.56
  69.7 1.3 fusion.55
  71.0 1.7 collective-permute-start.1
  72.7 1.1 convolution_bitcast_fusion.1
  73.8 0.7 copy-done.6
  75.6 1.2 gather_fusion.5
  76.8 1.0 fusion.90
  78.3 0.6 collective-permute-done.4
  78.9 0.9 fusion.86
  79.9 1.2 fusion.71
  81.1 1.2 fusion.70
  82.3 1.2 fusion.9
  83.5 1.2 fusion.8
  85.7 1.1 convolution_bitcast_fusion
  86.7 0.7 copy-done.7
  87.4 0.6 slice.549
  88.1 3.2 %collective-permute-done.2 = bf16[2,16,8,128]{3,1,2,0:T(8,128)(2,1)S(1)} collective-permute-done((bf16[2,16,8,128]{3,1,2,0:T(8,128)(2,1)S(1)}, bf16[2,16,8,128]{3,1,2,0:T(8,128)(2,1)S(1)}, u32[]{:S(2)}, u32[]{:S(2)}) %collective-permute-start.2) | collective-permute-done | bytes 65568 | tf_op jit(solution)/shard_map/ppermute | solution.py:13
  91.3 1.2 gather_fusion.6
  92.5 1.1 fusion.89
  93.6 1.3 convolution_bitcast_fusion.14
  94.9 1.3 convolution_bitcast_fusion.12
  96.2 0.9 fusion.85
  98.3 1.2 fusion.67
  100.8 0.6 stack.156
  102.9 1.3 fusion.76
  104.2 1.2 fusion.77
  105.4 1.2 fusion
  106.6 1.2 fusion.1
  108.8 27.4 %scatter_fusion.1 = bf16[2,16,1024]{1,0,2:T(2,128)(2,1)S(1)} fusion(bf16[2,16,1024]{1,0,2:T(2,128)(2,1)S(1)} %broadcast.39.clone.1, s32[1024]{0:T(1024)S(1)} %get-tuple-element.46, bf16[1024,2,16]{2,1,0:T(2,128)(2,1)S(1)} %bitcast.684), kind=kCustom, calls=%fused_computation.10 | custom fusion | bytes 200704 | tf_op jit(solution)/shard_map/scatter | solution.py:89
  136.2 1.0 copy.141
  137.2 1.3 convolution_bitcast_fusion.10
  140.1 27.4 %scatter_fusion = bf16[2,16,1024]{1,0,2:T(2,128)(2,1)S(1)} fusion(bf16[2,16,1024]{1,0,2:T(2,128)(2,1)S(1)} %broadcast.39.clone, s32[1024]{0:T(1024)S(1)} %get-tuple-element.46, bf16[1024,2,16]{2,1,0:T(2,128)(2,1)S(1)} %copy.100), kind=kCustom, calls=%fused_computation.9 | custom fusion | bytes 200704 | tf_op jit(solution)/shard_map/scatter | solution.py:88
  167.5 1.0 copy.140
  (162 shorter events, 19.9 us)
Async XLA Ops:
  7.2 95.7 %all-gather.2.cloned.1.call-start = ((), (), s32[]{:S(2)}) async-start(), calls=%async_computation | async-start | bytes 1572864 | tf_op jit(solution)/shard_map/all_gather | solution.py:78
  8.6 5.3 %copy-start.9 = (bf16[2,16,1024]{2,1,0:T(8,128)(2,1)S(1)}, bf16[2,16,1024]{2,1,0:T(8,128)(2,1)}, u32[]{:S(2)}) copy-start(bf16[2,16,1024]{2,1,0:T(8,128)(2,1)} %param.14) | copy-start | bytes 196612
  8.6 5.7 %copy-start.10 = (bf16[2,16,1024]{2,1,0:T(8,128)(2,1)S(1)}, bf16[2,16,1024]{2,1,0:T(8,128)(2,1)}, u32[]{:S(2)}) copy-start(bf16[2,16,1024]{2,1,0:T(8,128)(2,1)} %param.13) | copy-start | bytes 196612
  22.1 8.3 %copy-start.11 = (s32[6,8,2]{1,2,0:T(2,128)S(1)}, s32[6,8,2]{1,2,0:T(2,128)}, u32[]{:S(2)}) copy-start(s32[6,8,2]{1,2,0:T(2,128)} %param.16) | copy-start | bytes 1156
  29.6 9.7 %copy-start = (bf16[8,2,2,128,128]{4,3,1,0,2:T(8,128)(2,1)}, bf16[8,2,2,128,128]{4,3,1,0,2:T(8,128)(2,1)S(1)}, u32[]{:S(2)}) copy-start(bf16[8,2,2,128,128]{4,3,1,0,2:T(8,128)(2,1)S(1)} %get-tuple-element.49) | copy-start | bytes 3145732
  29.6 16.2 %copy-start.2 = (bf16[8,2,2,128,128]{4,3,1,0,2:T(8,128)(2,1)}, bf16[8,2,2,128,128]{4,3,1,0,2:T(8,128)(2,1)S(1)}, u32[]{:S(2)}) copy-start(bf16[8,2,2,128,128]{4,3,1,0,2:T(8,128)(2,1)S(1)} %get-tuple-element.50) | copy-start | bytes 3145732
  31.4 7.9 %copy-start.5 = (f32[2,16,16,128]{3,2,1,0:T(8,128)}, f32[2,16,16,128]{3,2,1,0:T(8,128)S(1)}, u32[]{:S(2)}) copy-start(f32[2,16,16,128]{3,2,1,0:T(8,128)S(1)} %convolution_bitcast_fusion.2) | copy-start | bytes 786436
  32.1 34.5 %collective-permute-start.3 = (bf16[2,16,8,128]{3,2,1,0:T(8,128)(2,1)}, bf16[2,16,8,128]{3,2,1,0:T(8,128)(2,1)}, u32[]{:S(2)}, u32[]{:S(2)}) collective-permute-start(bf16[2,16,8,128]{3,2,1,0:T(8,128)(2,1)} %slice.551), channel_id=1, source_target_pairs={{0,8},{1,9},{4,12},{5,13},{8,0},{9,1},{12,4},{13,5},{2,10},{3,11},... | collective-permute-start | bytes 196616 | tf_op jit(solution)/shard_map/ppermute | solution.py:13
  40.7 7.9 %copy-start.15 = (s32[8,2]{0,1:T(2,128)S(1)}, s32[8,2]{0,1:T(2,128)}, u32[]{:S(2)}) copy-start(s32[8,2]{0,1:T(2,128)} %param.18) | copy-start | bytes 196
  48.7 12.3 %collective-permute-start = (bf16[2,16,8,128]{3,1,2,0:T(8,128)(2,1)}, bf16[2,16,8,128]{3,1,2,0:T(8,128)(2,1)}, u32[]{:S(2)}, u32[]{:S(2)}) collective-permute-start(bf16[2,16,8,128]{3,1,2,0:T(8,128)(2,1)} %pad_maximum_fusion.12), channel_id=1, source_target_pairs={{0,1},{1,0},{4,5},{5,4},{8,9},{9,8},{12,13},{13,12},{2,3},{3,2},{6... | collective-permute-start | bytes 196616 | tf_op jit(solution)/shard_map/ppermute | solution.py:13
  63.1 13.7 %copy-start.17 = (pred[8,2]{1,0:T(8,128)(4,1)S(1)}, pred[8,2]{1,0:T(8,128)(4,1)}, u32[]{:S(2)}) copy-start(pred[8,2]{1,0:T(8,128)(4,1)} %copy.66) | copy-start | bytes 52
  71.0 4.6 %collective-permute-start.1 = (bf16[2,16,8,128]{3,1,2,0:T(8,128)(2,1)S(1)}, bf16[2,16,8,128]{3,1,2,0:T(8,128)(2,1)S(1)}, u32[]{:S(2)}, u32[]{:S(2)}) collective-permute-start(bf16[2,16,8,128]{3,1,2,0:T(8,128)(2,1)S(1)} %pad_maximum_fusion.13), channel_id=1, source_target_pairs={{0,4},{1,5},{4,0},{5,1},{8,12},{9,13},{12,8},{13,9},{2,6},{3,7},{6... | collective-permute-start | bytes 196616 | tf_op jit(solution)/shard_map/ppermute | solution.py:13
  73.8 0.7 copy-start.6
  74.5 4.4 %collective-permute-start.4 = (bf16[2,16,8,128]{3,2,1,0:T(8,128)(2,1)S(1)}, bf16[2,16,8,128]{3,2,1,0:T(8,128)(2,1)}, u32[]{:S(2)}, u32[]{:S(2)}) collective-permute-start(bf16[2,16,8,128]{3,2,1,0:T(8,128)(2,1)S(1)} %slice.550), channel_id=1, source_target_pairs={{0,4},{1,5},{4,0},{5,1},{8,12},{9,13},{12,8},{13,9},{2,6},{3,7},{6... | collective-permute-start | bytes 196616 | tf_op jit(solution)/shard_map/ppermute | solution.py:13
  78.0 19.9 %copy-start.14 = (s32[8,2]{0,1:T(2,128)S(1)}, s32[8,2]{0,1:T(2,128)}, u32[]{:S(2)}) copy-start(s32[8,2]{0,1:T(2,128)} %get-tuple-element.29) | copy-start | bytes 196
  84.8 15.3 %copy-start.13 = (s32[8,2]{0,1:T(2,128)S(1)}, s32[8,2]{0,1:T(2,128)}, u32[]{:S(2)}) copy-start(s32[8,2]{0,1:T(2,128)} %get-tuple-element.30) | copy-start | bytes 196
  85.3 15.2 %copy-start.1 = (bf16[8,2,2,128,128]{4,3,1,0,2:T(8,128)(2,1)S(1)}, bf16[8,2,2,128,128]{4,3,1,0,2:T(8,128)(2,1)}, u32[]{:S(2)}) copy-start(bf16[8,2,2,128,128]{4,3,1,0,2:T(8,128)(2,1)} %copy-done) | copy-start | bytes 3145732
  85.3 5.9 %collective-permute-start.2 = (bf16[2,16,8,128]{3,1,2,0:T(8,128)(2,1)S(1)}, bf16[2,16,8,128]{3,1,2,0:T(8,128)(2,1)S(1)}, u32[]{:S(2)}, u32[]{:S(2)}) collective-permute-start(bf16[2,16,8,128]{3,1,2,0:T(8,128)(2,1)S(1)} %pad_maximum_fusion.14), channel_id=1, source_target_pairs={{0,8},{1,9},{4,12},{5,13},{8,0},{9,1},{12,4},{13,5},{2,10},{3,11},... | collective-permute-start | bytes 196616 | tf_op jit(solution)/shard_map/ppermute | solution.py:13
  86.7 0.7 copy-start.7
  88.1 8.1 %collective-permute-start.5 = (bf16[2,16,8,128]{3,2,1,0:T(8,128)(2,1)}, bf16[2,16,8,128]{3,2,1,0:T(8,128)(2,1)}, u32[]{:S(2)}, u32[]{:S(2)}) collective-permute-start(bf16[2,16,8,128]{3,2,1,0:T(8,128)(2,1)} %slice.549), channel_id=1, source_target_pairs={{0,1},{1,0},{4,5},{5,4},{8,9},{9,8},{12,13},{13,12},{2,3},{3,2},{6... | collective-permute-start | bytes 196616 | tf_op jit(solution)/shard_map/ppermute | solution.py:13
  92.5 7.0 %copy-start.3 = (bf16[8,2,2,128,128]{4,3,1,0,2:T(8,128)(2,1)S(1)}, bf16[8,2,2,128,128]{4,3,1,0,2:T(8,128)(2,1)}, u32[]{:S(2)}) copy-start(bf16[8,2,2,128,128]{4,3,1,0,2:T(8,128)(2,1)} %copy-done.2) | copy-start | bytes 3145732
  97.3 5.2 %copy-start.12 = (s32[8,2]{0,1:T(2,128)S(1)}, s32[8,2]{0,1:T(2,128)}, u32[]{:S(2)}) copy-start(s32[8,2]{0,1:T(2,128)} %get-tuple-element.27) | copy-start | bytes 196
  99.5 8.4 %copy-start.16 = (s32[8,2]{0,1:T(2,128)S(1)}, s32[8,2]{0,1:T(2,128)}, u32[]{:S(2)}) copy-start(s32[8,2]{0,1:T(2,128)} %param.18) | copy-start | bytes 196
  101.9 37.5 %copy-start.8 = (bf16[1,16,1024]{2,1,0:T(8,128)(2,1)S(1)}, bf16[1,16,1024]{2,1,0:T(8,128)(2,1)}, u32[]{:S(2)}) copy-start(bf16[1,16,1024]{2,1,0:T(8,128)(2,1)} %stack.156) | copy-start | bytes 98308
  102.9 35.6 %copy-start.4 = (bf16[8,2,2,128,128]{4,3,1,0,2:T(8,128)(2,1)S(1)}, bf16[8,2,2,128,128]{4,3,1,0,2:T(8,128)(2,1)}, u32[]{:S(2)}) copy-start(bf16[8,2,2,128,128]{4,3,1,0,2:T(8,128)(2,1)} %all-gather.2.cloned.1.call-done) | copy-start | bytes 3145732
Sparse Core Ops, SparseCore 0:
  38.2 20.5 all-gather.1
where the time goes:
time: 177 us; the launch traced here: 175 us
  local copies, waits for them, and re-layouts  101 us (57%)
  matrix products  32.8 us (19%)
  other arithmetic  15.7 us (9%)
  between operations  14.7 us (8%)
  starting transfers between devices  6.58 us (4%)
  waiting for transfers between devices  4.41 us (2%)
    scatter x1, local copies, waits for them, and re-layouts, body(): jnp.zeros_like(sources).at[:, :, tree_order].set(adjoint_tree)  27.4 us
    scatter x1, local copies, waits for them, and re-layouts, body(): jnp.zeros_like(sources).at[:, :, tree_order].set(forward_tree)  27.4 us
    dot_general x28, matrix products, product(): jnp.einsum('cgs,gksr->cgkr', left_part, right_part, preferred_element_typ...  14.6 us
    dot_general x28, matrix products, product(): jnp.einsum('cgkr,gksr->cgs', left_part, right_part, preferred_element_typ...  14.2 us
    unnamed x47, local copies, waits for them, and re-layouts  11.1 us
    gather x9, local copies, waits for them, and re-layouts, apply_blocks(): chosen = jnp.take(candidates, chosen_slots, axis=2)  7.64 us
    ppermute x6, starting transfers between devices, partner_2(): return lax.ppermute(value, axis, pairs)  6.54 us
    slice x1, local copies, waits for them, and re-layouts, body(): factor_weight[level_id]  5.3 us
  transfers between devices with their start and end apart: 7, of which 3 were waited for; matrix products, arithmetic and copies ran while one was open for 33% of the time, Pallas kernels for 0%

commit v1 on v0

v1 whole, which is shorter than its diff:
```python
import functools

import jax
import jax.numpy as jnp
from jax import lax
from jax.experimental import pallas as pl
from jax.experimental.pallas import tpu as pltpu
from jax.sharding import PartitionSpec as P

BLK = 128
LOC = 3
BF = jnp.bfloat16
F32 = jnp.float32
MESH = pl.DeviceIdType.MESH


def flip(value, bit):
    return value + (1 - 2 * ((value // bit) % 2)) * bit


def partner_of(t):
    if t == 0:
        return {"half": flip(lax.axis_index("half"), 1)}
    return {"leaf": flip(lax.axis_index("leaf"), 2 ** (t - 1))}


def dot_nn(a, b):
    return lax.dot_general(a, b, (((1,), (0,)), ((), ())), preferred_element_type=F32)


def dot_nt(a, b):
    return lax.dot_general(a, b, (((1,), (1,)), ((), ())), preferred_element_type=F32)


def combine_forward(out, cols):
    real = out[:cols, :BLK] - out[cols:, BLK:]
    imag = out[cols:, :BLK] + out[:cols, BLK:]
    return jnp.concatenate([real, imag], axis=0)


def conj_rows(value, cols):
    real, imag = value[:cols], value[cols:]
    return jnp.concatenate(
        [jnp.concatenate([real, imag], axis=1), jnp.concatenate([imag, -real], axis=1)], axis=0
    )


def kernel(
    levels, nb, cols, near, n_rhs,
    src, prb, fw, pat, nw, nidx, order,
    out_f, out_a,
    wv, nwv, raw, perm, xt, vt, fl, fx, ff, bcur, contrib, aown, asend, arecv,
    nf, na, nsend, nret,
    wsem, nwsem, rawsem, xs_sem, xr_sem, fs_sem, fr_sem, as_sem, ar_sem, ns_sem, nr_sem,
):
    rows = nb * BLK
    height = 2 * cols
    tops = levels - LOC
    me_rhs = lax.axis_index("rhs")

    def peer(d):
        return {"rhs": lax.rem(me_rhs + d, n_rhs)}

    def origin(d):
        return {"rhs": lax.rem(me_rhs + n_rhs - d, n_rhs)}

    barrier = pltpu.get_barrier_semaphore()
    for t in range(tops):
        pl.semaphore_signal(barrier, inc=1, device_id=partner_of(t), device_id_type=MESH)
    for d in range(1, n_rhs):
        pl.semaphore_signal(barrier, inc=1, device_id=peer(d), device_id_type=MESH)

    raw_copies = [
        pltpu.make_async_copy(src, raw.at[0, 0], rawsem.at[0]),
        pltpu.make_async_copy(prb, raw.at[0, 1], rawsem.at[1]),
    ]
    for copy in raw_copies:
        copy.start()
    wcopies = [pltpu.make_async_copy(fw.at[l], wv.at[l], wsem.at[l]) for l in range(levels)]
    order_of_levels = []
    for l in range((levels + 1) // 2):
        for pick in (levels - 1 - l, l):
            if pick not in order_of_levels:
                order_of_levels.append(pick)
    for l in order_of_levels:
        wcopies[l].start()
    ncopy = pltpu.make_async_copy(nw, nwv, nwsem)
    ncopy.start()
    wready = set()

    def ready(l):
        if l not in wready:
            wcopies[l].wait()
            wready.add(l)

    pl.semaphore_wait(barrier, tops + n_rhs - 1)
    raw_sends = []
    for d in range(1, n_rhs):
        for which, ref in ((0, src), (1, prb)):
            copy = pltpu.make_async_remote_copy(
                src_ref=ref,
                dst_ref=raw.at[d, which],
                send_sem=xs_sem.at[d - 1, which],
                recv_sem=xr_sem.at[d - 1, which],
                device_id=peer(d),
                device_id_type=MESH,
            )
            copy.start()
            raw_sends.append(copy)

    wanted = [jnp.broadcast_to(order[q : q + 1, :], (16, BLK)) for q in range(nb)]
    step_iota = lax.broadcasted_iota(jnp.int32, (16, BLK), 0)

    def build(j, carry):
        base = pl.multiple_of(j * 16, 16)
        line = step_iota + base
        for q in range(nb):
            perm[pl.ds(base, 16), q * BLK : (q + 1) * BLK] = jnp.where(
                wanted[q] == line, 1.0, 0.0
            ).astype(BF)
        return carry

    lax.fori_loop(0, rows // 16, build, 0, unroll=4)

    def to_tree(d):
        stacked = jnp.concatenate(
            [raw[d, 0, 0], raw[d, 0, 1], raw[d, 1, 0], raw[d, 1, 1]], axis=0
        )
        for n in range(nb // 2):
            lo = n * 2 * BLK
            got = dot_nn(stacked, perm[:, lo : lo + 2 * BLK]).astype(BF)
            for e in range(2):
                xt[d, 2 * n + e] = got[:height, e * BLK : (e + 1) * BLK]
                vt[d, 2 * n + e] = got[height:, e * BLK : (e + 1) * BLK]

    def big(l, g):
        return jnp.concatenate(
            [wv[l, g, 0].reshape(2 * BLK, BLK), wv[l, g, 1].reshape(2 * BLK, BLK)], axis=1
        )

    def forward_level(l, cur, dst):
        ready(l)
        for g in range(nb):
            lhs = jnp.concatenate(
                [cur[pat[l, 0, g]], cur[pat[l, 1, g]]], axis=1
            )
            dst[g] = combine_forward(dot_nt(lhs, big(l, g)), cols).astype(BF)

    def masked_sum(pieces, spots, h):
        total = jnp.where(spots[0] == h, pieces[0], 0.0)
        for spot, piece in zip(spots[1:], pieces[1:]):
            total = total + jnp.where(spot == h, piece, 0.0)
        return total

    def adjoint_level(l, cur, dst):
        ready(l)
        for g in range(nb):
            out = dot_nn(conj_rows(cur[g], cols), big(l, g))
            contrib[2 * g] = out[:, :BLK]
            contrib[2 * g + 1] = out[:, BLK:]
        spots = [jnp.full((height, BLK), pat[l, j % 2, j // 2], jnp.int32) for j in range(2 * nb)]

        def sum_for(h):
            return masked_sum([contrib[j] for j in range(2 * nb)], spots, h)

        if l < LOC:

            def local(h, carry):
                dst[h] = sum_for(h).astype(BF)
                return carry

            lax.fori_loop(0, nb, local, 0)
            return None
        t = l - LOC

        def far(h, carry):
            asend[t, h] = sum_for(h + nb).astype(BF)
            return carry

        lax.fori_loop(0, nb, far, 0)
        copy = pltpu.make_async_remote_copy(
            src_ref=asend.at[t],
            dst_ref=arecv.at[t],
            send_sem=as_sem.at[t],
            recv_sem=ar_sem.at[t],
            device_id=partner_of(t),
            device_id_type=MESH,
        )
        copy.start()

        def own(h, carry):
            aown[h] = sum_for(h)
            return carry

        lax.fori_loop(0, nb, own, 0)
        return copy

    def adjoint_arrive(l, copy):
        copy.wait_recv()
        t = l - LOC
        for h in range(nb):
            bcur[l, h] = (aown[h] + arecv[t, h].astype(F32)).astype(BF)

    def forward_send(t):
        copy = pltpu.make_async_remote_copy(
            src_ref=fx[t].at[pl.ds(0, nb)],
            dst_ref=fx[t].at[pl.ds(nb, nb)],
            send_sem=fs_sem.at[t],
            recv_sem=fr_sem.at[t],
            device_id=partner_of(t),
            device_id_type=MESH,
        )
        copy.start()
        return copy

    def near_parts(d):
        m0 = me_rhs * near
        for g in range(nb):
            acc = None
            for m in range(near):
                got = dot_nt(xt[d, nidx[m0 + m, g]], nwv[g, m].reshape(2 * BLK, BLK))
                got = combine_forward(got, cols)
                acc = got if acc is None else acc + got
            if d == 0:
                nf[g] = acc
            else:
                nsend[d - 1, 0, g] = acc.astype(BF)
        for h in range(nb):
            na[h] = jnp.zeros((height, BLK), F32) if d == 0 else na[h]
        for m in range(near):
            for g in range(nb):
                contrib[g] = dot_nn(
                    conj_rows(vt[d, g], cols), nwv[g, m].reshape(2 * BLK, BLK)
                )
            spots = [jnp.full((height, BLK), nidx[m0 + m, g], jnp.int32) for g in range(nb)]

            def one(h, carry):
                total = masked_sum([contrib[g] for g in range(nb)], spots, h)
                if d == 0:
                    na[h] = na[h] + total
                elif near == 1:
                    nsend[d - 1, 1, h] = total.astype(BF)
                else:
                    before = nsend[d - 1, 1, h].astype(F32) if m else 0.0
                    nsend[d - 1, 1, h] = (before + total).astype(BF)
                return carry

            lax.fori_loop(0, nb, one, 0)

    for copy in raw_copies:
        copy.wait()
    to_tree(0)
    sends_a = {}
    sends_f = {}
    sends_a[levels - 1] = adjoint_level(levels - 1, vt.at[0], None)
    cur = xt.at[0]
    for l in range(LOC):
        dst = fx[0].at[pl.ds(0, nb)] if l == LOC - 1 else fl.at[l]
        forward_level(l, cur, dst)
        cur = dst
    sends_f[0] = forward_send(0)

    ncopy.wait()
    near_parts(0)
    near_sends = []
    for d in range(1, n_rhs):
        raw_sends[2 * (d - 1)].wait_recv()
        raw_sends[2 * (d - 1) + 1].wait_recv()
        to_tree(d)
        near_parts(d)
        copy = pltpu.make_async_remote_copy(
            src_ref=nsend.at[d - 1],
            dst_ref=nret.at[d - 1],
            send_sem=ns_sem.at[d - 1],
            recv_sem=nr_sem.at[d - 1],
            device_id=origin(d),
            device_id_type=MESH,
        )
        copy.start()
        near_sends.append(copy)

    for i in range(tops):
        sends_f[i].wait_recv()
        last = i == tops - 1
        forward_level(LOC + i, fx[i], ff if last else fx[i + 1].at[pl.ds(0, nb)])
        if not last:
            sends_f[i + 1] = forward_send(i + 1)
        la = levels - 1 - i
        adjoint_arrive(la, sends_a[la])
        if not last:
            sends_a[la - 1] = adjoint_level(la - 1, bcur.at[la], None)
    for l in reversed(range(LOC)):
        adjoint_level(l, bcur.at[l + 1], bcur.at[l])

    for copy in near_sends:
        copy.wait_recv()
    lines_f, lines_a = [], []
    for g in range(nb):
        tf, ta = nf[g], na[g]
        for d in range(1, n_rhs):
            tf = tf + nret[d - 1, 0, g].astype(F32)
            ta = ta + nret[d - 1, 1, g].astype(F32)
        lines_f.append((ff[g].astype(F32) + tf).astype(BF))
        lines_a.append((bcur[0, g].astype(F32) + ta).astype(BF))
    tree = jnp.concatenate(
        [jnp.concatenate(lines_f, axis=1), jnp.concatenate(lines_a, axis=1)], axis=0
    )
    for n in range(nb // 2):
        lo = n * 2 * BLK
        got = dot_nt(tree, perm[lo : lo + 2 * BLK, :]).astype(BF)
        for z in range(2):
            out_f[z, :, lo : lo + 2 * BLK] = got[z * cols : (z + 1) * cols]
            out_a[z, :, lo : lo + 2 * BLK] = got[height + z * cols : height + (z + 1) * cols]

    for copy in raw_sends + near_sends + list(sends_f.values()) + list(sends_a.values()):
        copy.wait_send()


def body(n_rhs, sources, probe_field, factor_weight, factor_pattern, near_weight, near_index, tree_order):
    columns = sources.shape[1]
    rows = sources.shape[2]
    cols = -(-columns // 16) * 16
    if cols != columns:
        widen = ((0, 0), (0, cols - columns), (0, 0))
        sources = jnp.pad(sources, widen)
        probe_field = jnp.pad(probe_field, widen)
    nb = rows // BLK
    levels = factor_weight.shape[0]
    tops = levels - LOC
    near = near_weight.shape[1]
    height = 2 * cols
    block = (height, BLK)
    others = n_rhs - 1
    dma = pltpu.SemaphoreType.DMA
    any_spec = pl.BlockSpec(memory_space=pltpu.HBM)
    smem = pl.BlockSpec(memory_space=pltpu.SMEM)
    vmem = pl.BlockSpec(memory_space=pltpu.VMEM)
    out = jax.ShapeDtypeStruct((2, cols, rows), BF)
    forward_field, adjoint_field = pl.pallas_call(
        functools.partial(kernel, levels, nb, cols, near, n_rhs),
        out_shape=(out, out),
        in_specs=[any_spec, any_spec, any_spec, smem, any_spec, smem, vmem],
        out_specs=(vmem, vmem),
        scratch_shapes=[
            pltpu.VMEM(factor_weight.shape, BF),
            pltpu.VMEM(near_weight.shape, BF),
            pltpu.VMEM((n_rhs, 2, 2, cols, rows), BF),
            pltpu.VMEM((rows, rows), BF),
            pltpu.VMEM((n_rhs, nb) + block, BF),
            pltpu.VMEM((n_rhs, nb) + block, BF),
            pltpu.VMEM((LOC, nb) + block, BF),
            [pltpu.VMEM((2 * nb,) + block, BF) for _ in range(tops)],
            pltpu.VMEM((nb,) + block, BF),
            pltpu.VMEM((levels, nb) + block, BF),
            pltpu.VMEM((2 * nb,) + block, F32),
            pltpu.VMEM((nb,) + block, F32),
            pltpu.VMEM((tops, nb) + block, BF),
            pltpu.VMEM((tops, nb) + block, BF),
            pltpu.VMEM((nb,) + block, F32),
            pltpu.VMEM((nb,) + block, F32),
            pltpu.VMEM((others, 2, nb) + block, BF),
            pltpu.VMEM((others, 2, nb) + block, BF),
            dma((levels,)),
            dma,
            dma((2,)),
            dma((others, 2)),
            dma((others, 2)),
            dma((tops,)),
            dma((tops,)),
            dma((tops,)),
            dma((tops,)),
            dma((others,)),
            dma((others,)),
        ],
        compiler_params=pltpu.CompilerParams(
            collective_id=0, has_side_effects=True, vmem_limit_bytes=60 * 2**20
        ),
    )(
        sources,
        probe_field,
        factor_weight,
        jnp.swapaxes(factor_pattern, 1, 2),
        near_weight,
        jnp.swapaxes(near_index, 0, 1),
        tree_order.reshape(nb, BLK),
    )
    return forward_field[:, :columns], adjoint_field[:, :columns]


def solution(mesh):
    rows = ("groups", "leaf", "half")
    return jax.shard_map(
        functools.partial(body, mesh.shape["rhs"]),
        mesh=mesh,
        in_specs=(
            P(None, "rhs", rows),
            P(None, "rhs", rows),
            P(None, rows, None, None, None, None),
            P(None, rows, None),
            P(rows, "rhs", None, None, None),
            P(rows, None),
            P(rows),
        ),
        out_specs=(P(None, "rhs", rows), P(None, "rhs", rows)),
        check_vma=False,
    )
```

time: 177 us -> 27.3 us (0.15)
  local copies, waits for them, and re-layouts: 101 us -> 2.95 us
  matrix products: 32.8 us -> 0 us
  Pallas kernels: 0 us -> 23.5 us
  other arithmetic: 15.7 us -> 0 us
  between operations: 14.7 us -> 0.64 us
  starting transfers between devices: 6.58 us -> 0 us
  waiting for transfers between devices: 4.41 us -> 0 us
    scatter x2 -> x0, local copies, waits for them, and re-layouts: 54.8 us -> none  [the longest x1 27.4 us: body(): jnp.zeros_like(sources).at[:, :, tree_order].set(adjoint_tree)]
    dot_general x63 -> x0, matrix products: 32.8 us -> none  [the longest x28 14.6 us: product(): jnp.einsum('cgs,gksr->cgkr', left_part, right_part, preferred_element_typ...]
    pallas_call x0 -> x1, Pallas kernels: none -> 23.5 us  [body(): pl.pallas_call(functools.partial(kernel, levels, nb, cols, near, n_rhs),...]
    gather x11 -> x0, local copies, waits for them, and re-layouts: 15 us -> none  [the longest x9 7.64 us: apply_blocks(): chosen = jnp.take(candidates, chosen_slots, axis=2)]
    select_n x10 -> x0, other arithmetic: 8.46 us -> none  [the longest x1 4.46 us: body(): v_tree = jnp.take(probe_field, tree_order, axis=2)]
    unnamed x47 -> x2, local copies, waits for them, and re-layouts: 11.1 us -> 2.95 us
    slice x7 -> x0, local copies, waits for them, and re-layouts: 7.87 us -> none  [the longest x1 5.3 us: body(): factor_weight[level_id]]
    ppermute x6 -> x0, starting transfers between devices: 6.54 us -> none  [partner_2(): return lax.ppermute(value, axis, pairs)]
  transfers between devices with their start and end apart: 7 -> 0, of which waited for: 3 -> 0; matrix products, arithmetic and copies ran while one was open for 33% -> 0% of each run, Pallas kernels for 0% -> 0%
where the time goes in v1:
time: 27.3 us; the launch traced here: 27.1 us
  Pallas kernels  23.5 us (86%)
  local copies, waits for them, and re-layouts  2.95 us (11%)
  between operations  0.64 us (2%)
    pallas_call x1, Pallas kernels, body(): pl.pallas_call(functools.partial(kernel, levels, nb, cols, near, n_rhs),...  23.5 us
    unnamed x2, local copies, waits for them, and re-layouts  2.95 us

profile of v1, /device:TPU:0, one launch (start us, length us, event | category | flops | bytes accessed | tf_op | source)
XLA Modules:
  0.0 27.1 jit_solution(14083441247369639670)
XLA Ops:
  0.6 23.5 %shard_map.86 = (bf16[2,16,1024]{2,1,0:T(8,128)(2,1)}, bf16[2,16,1024]{2,1,0:T(8,128)(2,1)}) custom-call(bf16[2,16,1024]{2,1,0:T(8,128)(2,1)} %src.1, bf16[2,16,1024]{2,1,0:T(8,128)(2,1)} %prb.1, bf16[6,8,2,2,128,128]{5,4,3,2,1,0:T(8,128)(2,1)} %fw.1, s32[6,2,8]{2,1,0:T(2,128)} %bitcast.3, bf16[8,1,2,128,128]{4,3,2,1,0:T(8,128)(2,1)} %nw.1, s32[2,8]{1,0:T(2,128)} %bitcast.5, ...), custom_call_target="tpu_custom_call" | custom-call | tf_op jit(solution)/shard_map/pallas_call | solution.py:339
  24.1 1.5 %copy.11 = bf16[2,16,1024]{2,1,0:T(8,128)(2,1)} copy(bf16[2,16,1024]{2,1,0:T(8,128)(2,1)} %get-tuple-element.4) | data formatting | bytes 131072
  25.6 1.5 %copy.12 = bf16[2,16,1024]{2,1,0:T(8,128)(2,1)} copy(bf16[2,16,1024]{2,1,0:T(8,128)(2,1)} %get-tuple-element.5) | data formatting | bytes 131072

commit v2 on v1

--- a/solution.py
+++ b/solution.py
@@ -48,7 +48,7 @@
 def kernel(
     levels, nb, cols, near, n_rhs,
     src, prb, fw, pat, nw, nidx, order,
-    out_f, out_a,
+    out,
     wv, nwv, raw, perm, xt, vt, fl, fx, ff, bcur, contrib, aown, asend, arecv,
     nf, na, nsend, nret,
     wsem, nwsem, rawsem, xs_sem, xr_sem, fs_sem, fr_sem, as_sem, ar_sem, ns_sem, nr_sem,
@@ -77,36 +77,19 @@
     for copy in raw_copies:
         copy.start()
     wcopies = [pltpu.make_async_copy(fw.at[l], wv.at[l], wsem.at[l]) for l in range(levels)]
-    order_of_levels = []
-    for l in range((levels + 1) // 2):
-        for pick in (levels - 1 - l, l):
-            if pick not in order_of_levels:
-                order_of_levels.append(pick)
-    for l in order_of_levels:
+    ncopy = pltpu.make_async_copy(nw, nwv, nwsem)
+    first = [levels - 1] + list(range(LOC))
+    for l in first:
         wcopies[l].start()
-    ncopy = pltpu.make_async_copy(nw, nwv, nwsem)
     ncopy.start()
+    for l in range(LOC, levels - 1):
+        wcopies[l].start()
     wready = set()
 
     def ready(l):
         if l not in wready:
             wcopies[l].wait()
             wready.add(l)
-
-    pl.semaphore_wait(barrier, tops + n_rhs - 1)
-    raw_sends = []
-    for d in range(1, n_rhs):
-        for which, ref in ((0, src), (1, prb)):
-            copy = pltpu.make_async_remote_copy(
-                src_ref=ref,
-                dst_ref=raw.at[d, which],
-                send_sem=xs_sem.at[d - 1, which],
-                recv_sem=xr_sem.at[d - 1, which],
-                device_id=peer(d),
-                device_id_type=MESH,
-            )
-            copy.start()
-            raw_sends.append(copy)
 
     wanted = [jnp.broadcast_to(order[q : q + 1, :], (16, BLK)) for q in range(nb)]
     step_iota = lax.broadcasted_iota(jnp.int32, (16, BLK), 0)
@@ -173,6 +156,10 @@
             return None
         t = l - LOC
 
+        def own(h, carry):
+            aown[h] = sum_for(h)
+            return carry
+
         def far(h, carry):
             asend[t, h] = sum_for(h + nb).astype(BF)
             return carry
@@ -187,11 +174,6 @@
             device_id_type=MESH,
         )
         copy.start()
-
-        def own(h, carry):
-            aown[h] = sum_for(h)
-            return carry
-
         lax.fori_loop(0, nb, own, 0)
         return copy
 
@@ -210,7 +192,6 @@
             device_id=partner_of(t),
             device_id_type=MESH,
         )
-        copy.start()
         return copy
 
     def near_parts(d):
@@ -250,6 +231,20 @@
     for copy in raw_copies:
         copy.wait()
     to_tree(0)
+    pl.semaphore_wait(barrier, tops + n_rhs - 1)
+    raw_sends = []
+    for d in range(1, n_rhs):
+        for which, ref in ((0, src), (1, prb)):
+            copy = pltpu.make_async_remote_copy(
+                src_ref=ref,
+                dst_ref=raw.at[d, which],
+                send_sem=xs_sem.at[d - 1, which],
+                recv_sem=xr_sem.at[d - 1, which],
+                device_id=peer(d),
+                device_id_type=MESH,
+            )
+            copy.start()
+            raw_sends.append(copy)
     sends_a = {}
     sends_f = {}
     sends_a[levels - 1] = adjoint_level(levels - 1, vt.at[0], None)
@@ -259,38 +254,41 @@
         forward_level(l, cur, dst)
         cur = dst
     sends_f[0] = forward_send(0)
-
+    sends_f[0].start()
     ncopy.wait()
     near_parts(0)
     near_sends = []
-    for d in range(1, n_rhs):
-        raw_sends[2 * (d - 1)].wait_recv()
-        raw_sends[2 * (d - 1) + 1].wait_recv()
-        to_tree(d)
-        near_parts(d)
-        copy = pltpu.make_async_remote_copy(
-            src_ref=nsend.at[d - 1],
-            dst_ref=nret.at[d - 1],
-            send_sem=ns_sem.at[d - 1],
-            recv_sem=nr_sem.at[d - 1],
-            device_id=origin(d),
-            device_id_type=MESH,
-        )
-        copy.start()
-        near_sends.append(copy)
-
     for i in range(tops):
         sends_f[i].wait_recv()
         last = i == tops - 1
         forward_level(LOC + i, fx[i], ff if last else fx[i + 1].at[pl.ds(0, nb)])
         if not last:
             sends_f[i + 1] = forward_send(i + 1)
-        la = levels - 1 - i
-        adjoint_arrive(la, sends_a[la])
+            sends_f[i + 1].start()
+        if i == 0:
+            for d in range(1, n_rhs):
+                raw_sends[2 * (d - 1)].wait_recv()
+                raw_sends[2 * (d - 1) + 1].wait_recv()
+                to_tree(d)
+                near_parts(d)
+                copy = pltpu.make_async_remote_copy(
+                    src_ref=nsend.at[d - 1],
+                    dst_ref=nret.at[d - 1],
+                    send_sem=ns_sem.at[d - 1],
+                    recv_sem=nr_sem.at[d - 1],
+                    device_id=origin(d),
+                    device_id_type=MESH,
+                )
+                copy.start()
+                near_sends.append(copy)
         if not last:
+            la = levels - 1 - i
+            adjoint_arrive(la, sends_a[la])
             sends_a[la - 1] = adjoint_level(la - 1, bcur.at[la], None)
-    for l in reversed(range(LOC)):
-        adjoint_level(l, bcur.at[l + 1], bcur.at[l])
+        if i == tops - 2:
+            adjoint_arrive(LOC, sends_a[LOC])
+            for l in reversed(range(LOC)):
+                adjoint_level(l, bcur.at[l + 1], bcur.at[l])
 
     for copy in near_sends:
         copy.wait_recv()
@@ -309,8 +307,8 @@
         lo = n * 2 * BLK
         got = dot_nt(tree, perm[lo : lo + 2 * BLK, :]).astype(BF)
         for z in range(2):
-            out_f[z, :, lo : lo + 2 * BLK] = got[z * cols : (z + 1) * cols]
-            out_a[z, :, lo : lo + 2 * BLK] = got[height + z * cols : height + (z + 1) * cols]
+            out[0, z, :, lo : lo + 2 * BLK] = got[z * cols : (z + 1) * cols]
+            out[1, z, :, lo : lo + 2 * BLK] = got[height + z * cols : height + (z + 1) * cols]
 
     for copy in raw_sends + near_sends + list(sends_f.values()) + list(sends_a.values()):
         copy.wait_send()
@@ -336,11 +334,11 @@
     smem = pl.BlockSpec(memory_space=pltpu.SMEM)
     vmem = pl.BlockSpec(memory_space=pltpu.VMEM)
     out = jax.ShapeDtypeStruct((2, cols, rows), BF)
-    forward_field, adjoint_field = pl.pallas_call(
+    both = pl.pallas_call(
         functools.partial(kernel, levels, nb, cols, near, n_rhs),
-        out_shape=(out, out),
+        out_shape=jax.ShapeDtypeStruct((2, 2, cols, rows), BF),
         in_specs=[any_spec, any_spec, any_spec, smem, any_spec, smem, vmem],
-        out_specs=(vmem, vmem),
+        out_specs=vmem,
         scratch_shapes=[
             pltpu.VMEM(factor_weight.shape, BF),
             pltpu.VMEM(near_weight.shape, BF),
@@ -384,6 +382,7 @@
         jnp.swapaxes(near_index, 0, 1),
         tree_order.reshape(nb, BLK),
     )
+    forward_field, adjoint_field = both[0], both[1]
     return forward_field[:, :columns], adjoint_field[:, :columns]
 
 

time: 27.3 us -> 24.5 us (0.90)
  local copies, waits for them, and re-layouts: 2.95 us -> 1.53 us
  Pallas kernels: 23.5 us -> 22.2 us
    unnamed x2 -> x0, local copies, waits for them, and re-layouts: 2.95 us -> none
    squeeze x0 -> x1, local copies, waits for them, and re-layouts: none -> 1.53 us  [body(): forward_field, adjoint_field = (both[0], both[1])]
    pallas_call x1, Pallas kernels: 23.5 us -> 22.2 us  [body(): pl.pallas_call(functools.partial(kernel, levels, nb, cols, near, n_rhs),...]
where the time goes in v2:
time: 24.5 us; the launch traced here: 24.3 us
  Pallas kernels  22.2 us (91%)
  local copies, waits for them, and re-layouts  1.53 us (6%)
  between operations  0.64 us (3%)
    pallas_call x1, Pallas kernels, body(): pl.pallas_call(functools.partial(kernel, levels, nb, cols, near, n_rhs),...  22.2 us
    squeeze x1, local copies, waits for them, and re-layouts, body(): forward_field, adjoint_field = (both[0], both[1])  1.53 us

profile of v2, /device:TPU:0, one launch (start us, length us, event | category | flops | bytes accessed | tf_op | source)
XLA Modules:
  0.0 24.3 jit_solution(15543434858192192938)
XLA Ops:
  0.6 22.2 %shard_map.86 = bf16[2,2,16,1024]{3,2,1,0:T(8,128)(2,1)} custom-call(bf16[2,16,1024]{2,1,0:T(8,128)(2,1)} %src.1, bf16[2,16,1024]{2,1,0:T(8,128)(2,1)} %prb.1, bf16[6,8,2,2,128,128]{5,4,3,2,1,0:T(8,128)(2,1)} %fw.1, s32[6,2,8]{2,1,0:T(2,128)} %bitcast.7, bf16[8,1,2,128,128]{4,3,2,1,0:T(8,128)(2,1)} %nw.1, s32[2,8]{1,0:T(2,128)} %bitcast.9, s32[8,128]{1,0:T(8,128)} %bitcast.8), custom_call_target="tpu_custom_call" | custom-call | tf_op jit(solution)/shard_map/pallas_call | solution.py:337
  22.8 1.5 %slice_bitcast_fusion = (bf16[2,16,1024]{2,1,0:T(8,128)(2,1)}, bf16[2,16,1024]{2,1,0:T(8,128)(2,1)}) fusion(bf16[2,2,16,1024]{3,2,1,0:T(8,128)(2,1)} %shard_map.86), kind=kLoop, calls=%fused_computation | loop fusion | bytes 262144 | tf_op jit(solution)/shard_map/squeeze | solution.py:385

commit v3 on v2

--- a/solution.py
+++ b/solution.py
@@ -47,15 +47,16 @@
 
 def kernel(
     levels, nb, cols, near, n_rhs,
-    src, prb, fw, pat, nw, nidx, order,
+    src, prb, fw, pat_hbm, nw, nidx_hbm, order_hbm,
     out,
-    wv, nwv, raw, perm, xt, vt, fl, fx, ff, bcur, contrib, aown, asend, arecv,
+    pat, nidx, order, small_sem, wv, nwv, raw, perm, xt, vt, fl, fx, ff, bcur, contrib, aown, asend, arecv,
     nf, na, nsend, nret,
     wsem, nwsem, rawsem, xs_sem, xr_sem, fs_sem, fr_sem, as_sem, ar_sem, ns_sem, nr_sem,
 ):
     rows = nb * BLK
     height = 2 * cols
     tops = levels - LOC
+    half = nb // 2
     me_rhs = lax.axis_index("rhs")
 
     def peer(d):
@@ -70,6 +71,13 @@
     for d in range(1, n_rhs):
         pl.semaphore_signal(barrier, inc=1, device_id=peer(d), device_id_type=MESH)
 
+    small_copies = [
+        pltpu.make_async_copy(order_hbm, order, small_sem.at[0]),
+        pltpu.make_async_copy(pat_hbm, pat, small_sem.at[1]),
+        pltpu.make_async_copy(nidx_hbm, nidx, small_sem.at[2]),
+    ]
+    for copy in small_copies:
+        copy.start()
     raw_copies = [
         pltpu.make_async_copy(src, raw.at[0, 0], rawsem.at[0]),
         pltpu.make_async_copy(prb, raw.at[0, 1], rawsem.at[1]),
@@ -91,6 +99,7 @@
             wcopies[l].wait()
             wready.add(l)
 
+    small_copies[0].wait()
     wanted = [jnp.broadcast_to(order[q : q + 1, :], (16, BLK)) for q in range(nb)]
     step_iota = lax.broadcasted_iota(jnp.int32, (16, BLK), 0)
 
@@ -121,13 +130,15 @@
             [wv[l, g, 0].reshape(2 * BLK, BLK), wv[l, g, 1].reshape(2 * BLK, BLK)], axis=1
         )
 
-    def forward_level(l, cur, dst):
+    def forward_level(l, cur, dst, after=None):
         ready(l)
         for g in range(nb):
             lhs = jnp.concatenate(
                 [cur[pat[l, 0, g]], cur[pat[l, 1, g]]], axis=1
             )
             dst[g] = combine_forward(dot_nt(lhs, big(l, g)), cols).astype(BF)
+            if after is not None and (g + 1) % half == 0:
+                after[g // half].start()
 
     def masked_sum(pieces, spots, h):
         total = jnp.where(spots[0] == h, pieces[0], 0.0)
@@ -164,35 +175,42 @@
             asend[t, h] = sum_for(h + nb).astype(BF)
             return carry
 
-        lax.fori_loop(0, nb, far, 0)
-        copy = pltpu.make_async_remote_copy(
-            src_ref=asend.at[t],
-            dst_ref=arecv.at[t],
-            send_sem=as_sem.at[t],
-            recv_sem=ar_sem.at[t],
-            device_id=partner_of(t),
-            device_id_type=MESH,
-        )
-        copy.start()
+        copies = []
+        for e in range(2):
+            lax.fori_loop(e * half, (e + 1) * half, far, 0)
+            part = pl.ds(e * half, half)
+            copy = pltpu.make_async_remote_copy(
+                src_ref=asend.at[t, part],
+                dst_ref=arecv.at[t, part],
+                send_sem=as_sem.at[t, e],
+                recv_sem=ar_sem.at[t, e],
+                device_id=partner_of(t),
+                device_id_type=MESH,
+            )
+            copy.start()
+            copies.append(copy)
         lax.fori_loop(0, nb, own, 0)
-        return copy
-
-    def adjoint_arrive(l, copy):
-        copy.wait_recv()
+        return copies
+
+    def adjoint_arrive(l, copies):
         t = l - LOC
         for h in range(nb):
+            if h % half == 0:
+                copies[h // half].wait_recv()
             bcur[l, h] = (aown[h] + arecv[t, h].astype(F32)).astype(BF)
 
     def forward_send(t):
-        copy = pltpu.make_async_remote_copy(
-            src_ref=fx[t].at[pl.ds(0, nb)],
-            dst_ref=fx[t].at[pl.ds(nb, nb)],
-            send_sem=fs_sem.at[t],
-            recv_sem=fr_sem.at[t],
-            device_id=partner_of(t),
-            device_id_type=MESH,
-        )
-        return copy
+        return [
+            pltpu.make_async_remote_copy(
+                src_ref=fx[t].at[pl.ds(e * half, half)],
+                dst_ref=fx[t].at[pl.ds(nb + e * half, half)],
+                send_sem=fs_sem.at[t, e],
+                recv_sem=fr_sem.at[t, e],
+                device_id=partner_of(t),
+                device_id_type=MESH,
+            )
+            for e in range(2)
+        ]
 
     def near_parts(d):
         m0 = me_rhs * near
@@ -245,27 +263,29 @@
             )
             copy.start()
             raw_sends.append(copy)
+    small_copies[1].wait()
+    small_copies[2].wait()
     sends_a = {}
     sends_f = {}
     sends_a[levels - 1] = adjoint_level(levels - 1, vt.at[0], None)
     cur = xt.at[0]
     for l in range(LOC):
         dst = fx[0].at[pl.ds(0, nb)] if l == LOC - 1 else fl.at[l]
-        forward_level(l, cur, dst)
+        if l == LOC - 1:
+            sends_f[0] = forward_send(0)
+        forward_level(l, cur, dst, sends_f.get(0))
         cur = dst
-    sends_f[0] = forward_send(0)
-    sends_f[0].start()
-    ncopy.wait()
-    near_parts(0)
     near_sends = []
     for i in range(tops):
-        sends_f[i].wait_recv()
+        for copy in sends_f[i]:
+            copy.wait_recv()
         last = i == tops - 1
-        forward_level(LOC + i, fx[i], ff if last else fx[i + 1].at[pl.ds(0, nb)])
         if not last:
             sends_f[i + 1] = forward_send(i + 1)
-            sends_f[i + 1].start()
+        forward_level(LOC + i, fx[i], ff if last else fx[i + 1].at[pl.ds(0, nb)], sends_f.get(i + 1))
         if i == 0:
+            ncopy.wait()
+            near_parts(0)
             for d in range(1, n_rhs):
                 raw_sends[2 * (d - 1)].wait_recv()
                 raw_sends[2 * (d - 1) + 1].wait_recv()
@@ -310,7 +330,8 @@
             out[0, z, :, lo : lo + 2 * BLK] = got[z * cols : (z + 1) * cols]
             out[1, z, :, lo : lo + 2 * BLK] = got[height + z * cols : height + (z + 1) * cols]
 
-    for copy in raw_sends + near_sends + list(sends_f.values()) + list(sends_a.values()):
+    level_sends = [c for pair in list(sends_f.values()) + list(sends_a.values()) for c in pair]
+    for copy in raw_sends + near_sends + level_sends:
         copy.wait_send()
 
 
@@ -331,15 +352,18 @@
     others = n_rhs - 1
     dma = pltpu.SemaphoreType.DMA
     any_spec = pl.BlockSpec(memory_space=pltpu.HBM)
-    smem = pl.BlockSpec(memory_space=pltpu.SMEM)
     vmem = pl.BlockSpec(memory_space=pltpu.VMEM)
     out = jax.ShapeDtypeStruct((2, cols, rows), BF)
     both = pl.pallas_call(
         functools.partial(kernel, levels, nb, cols, near, n_rhs),
         out_shape=jax.ShapeDtypeStruct((2, 2, cols, rows), BF),
-        in_specs=[any_spec, any_spec, any_spec, smem, any_spec, smem, vmem],
+        in_specs=[any_spec] * 7,
         out_specs=vmem,
         scratch_shapes=[
+            pltpu.SMEM((levels, 2, nb), jnp.int32),
+            pltpu.SMEM((near_index.shape[1], nb), jnp.int32),
+            pltpu.VMEM((nb, BLK), jnp.int32),
+            dma((3,)),
             pltpu.VMEM(factor_weight.shape, BF),
             pltpu.VMEM(near_weight.shape, BF),
             pltpu.VMEM((n_rhs, 2, 2, cols, rows), BF),
@@ -363,10 +387,10 @@
             dma((2,)),
             dma((others, 2)),
             dma((others, 2)),
-            dma((tops,)),
-            dma((tops,)),
-            dma((tops,)),
-            dma((tops,)),
+            dma((tops, 2)),
+            dma((tops, 2)),
+            dma((tops, 2)),
+            dma((tops, 2)),
             dma((others,)),
             dma((others,)),
         ],

time: 24.5 us -> 23.9 us (0.976)
  Pallas kernels: 22.2 us -> 21.6 us
    pallas_call x1, Pallas kernels: 22.2 us -> 21.6 us  [body(): pl.pallas_call(functools.partial(kernel, levels, nb, cols, near, n_rhs),...]
where the time goes in v3:
time: 23.9 us; the launch traced here: 23.8 us
  Pallas kernels  21.6 us (90%)
  local copies, waits for them, and re-layouts  1.53 us (6%)
  between operations  0.64 us (3%)
    pallas_call x1, Pallas kernels, body(): pl.pallas_call(functools.partial(kernel, levels, nb, cols, near, n_rhs),...  21.6 us
    squeeze x1, local copies, waits for them, and re-layouts, body(): forward_field, adjoint_field = (both[0], both[1])  1.53 us

profile of v3, /device:TPU:0, one launch (start us, length us, event | category | flops | bytes accessed | tf_op | source)
XLA Modules:
  0.0 23.8 jit_solution(10359626818234901826)
XLA Ops:
  0.6 21.6 %shard_map.86 = bf16[2,2,16,1024]{3,2,1,0:T(8,128)(2,1)} custom-call(bf16[2,16,1024]{2,1,0:T(8,128)(2,1)} %src.1, bf16[2,16,1024]{2,1,0:T(8,128)(2,1)} %prb.1, bf16[6,8,2,2,128,128]{5,4,3,2,1,0:T(8,128)(2,1)} %fw.1, s32[6,2,8]{2,1,0:T(2,128)} %bitcast.7, bf16[8,1,2,128,128]{4,3,2,1,0:T(8,128)(2,1)} %nw.1, s32[2,8]{1,0:T(2,128)} %bitcast.9, s32[8,128]{1,0:T(8,128)} %bitcast.8), custom_call_target="tpu_custom_call" | custom-call | tf_op jit(solution)/shard_map/pallas_call | solution.py:357
  22.3 1.5 %slice_bitcast_fusion = (bf16[2,16,1024]{2,1,0:T(8,128)(2,1)}, bf16[2,16,1024]{2,1,0:T(8,128)(2,1)}) fusion(bf16[2,2,16,1024]{3,2,1,0:T(8,128)(2,1)} %shard_map.86), kind=kLoop, calls=%fused_computation | loop fusion | bytes 262144 | tf_op jit(solution)/shard_map/squeeze | solution.py:409
